TPU v7x, 32 devices: a whole 2x2x4 slice. The times are simulated.
32 devices in a mesh: freq: 4 (over y, x), rcv: 8 (over z, core).
Axes of the slice: x: 2, y: 2, z: 4, core: 2. Of those that a mesh axis runs over, the one named last changes fastest.
Arguments:
- up_time: bfloat16 [32, 256, 20480], P(('freq', 'rcv')), may hold values from -74 to 74
- down_blocks: bfloat16 [8, 160, 11, 2, 128, 128], P('freq', 'rcv'), may hold values from -0.09375 to 0.09375
- block_cols: int32 [8, 160, 11], P('freq', 'rcv'), may hold values from 0 to 159, as said below
- block_counts: int32 [8, 160], P('freq', 'rcv'), may hold values from 1 to 11, as said below
Outputs:
- solution: float32 [2, 8, 32, 20480], P(None, 'freq', None, 'rcv')
- normal_residual: float32 [2, 8, 32, 20480], P(None, 'freq', None, 'rcv')
Inputs may be any that keep to these rules, and one draw needn't show every extreme that they name: block_cols[f, r, s] is the column block of slot s of row block r at frequency f; it differs from r by at most 5. Row block r of frequency f stores blocks in its first block_counts[f, r] slots.
All inputs are finite; a program needn't handle non-finite values.
Results may differ from a plain program's by a relative error of at most 0.0062.
Values may be sent and summed in bfloat16 or wider, within the bound.
A program may use at most 192 MiB of HBM per device.

v0:
```python
import functools
import math

import jax
import jax.numpy as jnp
from jax import lax
from jax.experimental import pallas as pl
from jax.experimental.pallas import tpu as pltpu
from jax.sharding import PartitionSpec as P

ITERS = 2
EPSILON = 1e-06
GROUP = 4


def fourier_table(time_steps, freqs):
    shape = (time_steps, freqs)
    sample = lax.broadcasted_iota(jnp.int32, shape, 0)
    harmonic = lax.broadcasted_iota(jnp.int32, shape, 1) + 1
    phase_angle = 2.0 * math.pi / time_steps * (harmonic * sample % time_steps).astype(jnp.float32)
    scale_factor = 1.0 / math.sqrt(time_steps)
    return jnp.stack(
        [jnp.cos(phase_angle) * scale_factor, -jnp.sin(phase_angle) * scale_factor], axis=1
    ).astype(jnp.bfloat16)


def pass_kernel(first, dims, *refs):
    freqs, rows, slots, blk, reach, sources = dims
    if first:
        counts, cols, blocks, start, t, psq, buf, lhs, item_row, item_f, item_a, item_b, item_buf, sems = refs
    else:
        (counts, cols, scale, blocks, field, prev, p_out, t, psq,
         buf, lhs, item_row, item_f, item_a, item_b, item_buf, sems, zb, acc) = refs
    span = rows + 2 * reach
    pairs = (slots + 1) // 2
    total_rows = freqs * rows
    base = lax.axis_index("rcv") * rows - reach

    def lanes(index):
        return pl.ds(pl.multiple_of(index * blk, blk), blk)

    def copy_of(f, r, s0, item):
        return pltpu.make_async_copy(
            blocks.at[f, r, pl.ds(s0, 2)], buf.at[item], sems.at[item // GROUP]
        )

    total = jnp.int32(0)
    for f in range(freqs):
        def each_row(r, n, f=f):
            fr = f * rows + r
            count = counts[fr]
            here = (count + 1) // 2

            def each_pair(k, carry):
                item = n + k
                s0 = jnp.minimum(2 * k, slots - 2)
                copy_of(f, r, s0, item).start()
                item_row[item] = fr
                item_f[item] = f
                item_buf[item] = item
                item_a[item] = jnp.where(s0 == 2 * k, cols[fr * slots + s0] - base, span)
                item_b[item] = jnp.where(s0 + 1 < count, cols[fr * slots + s0 + 1] - base, span)
                return carry

            lax.fori_loop(0, here, each_pair, 0)
            return n + here

        total = lax.fori_loop(0, rows, each_row, total)
    for j in range(GROUP):
        item_row[total + j] = total_rows
        item_f[total + j] = 0
        item_buf[total + j] = 0
        item_a[total + j] = span
        item_b[total + j] = span
    groups = (total + GROUP - 1) // GROUP

    def arrive(g):
        for j in range(GROUP):
            @pl.when(g * GROUP + j < total)
            def _():
                copy_of(0, 0, 0, g * GROUP + j).wait()

    t[...] = jnp.zeros_like(t)
    lhs[total_rows] = jnp.zeros(lhs.shape[1:], lhs.dtype)
    if not first:
        zb[:, :, :, : span * blk] = field[...].astype(jnp.bfloat16)
        zb[:, :, :, span * blk :] = jnp.zeros((2, freqs, sources, blk), jnp.bfloat16)
        acc[...] = jnp.zeros_like(acc)

        def forward(g, carry):
            arrive(g)
            for j in range(GROUP):
                i = g * GROUP + j
                f = item_f[i]
                za = zb[:, f, :, lanes(item_a[i])].reshape(2 * sources, blk)
                zc = zb[:, f, :, lanes(item_b[i])].reshape(2 * sources, blk)
                weights = buf[item_buf[i]].reshape(2, 2 * blk, blk)
                out = lax.dot_general(
                    jnp.concatenate([za, zc], axis=1),
                    jnp.concatenate([weights[0], weights[1]], axis=1),
                    (((1,), (1,)), ((), ())),
                    preferred_element_type=jnp.float32,
                )
                acc[item_row[i]] += out
            return carry

        lax.fori_loop(0, groups, forward, 0)

    for f in range(freqs):
        def finish(r, sums, f=f):
            fr = f * rows + r
            if first:
                real = start[0, f, :, lanes(r)]
                imag = start[1, f, :, lanes(r)]
                real16, imag16 = real, imag
                real, imag = real.astype(jnp.float32), imag.astype(jnp.float32)
            else:
                a = acc[fr]
                real = (
                    field[0, f, :, lanes(r + reach)]
                    + (a[:sources, :blk] - a[sources:, blk:])
                    - scale[f] * prev[0, f, :, lanes(r)]
                )
                imag = (
                    field[1, f, :, lanes(r + reach)]
                    + (a[:sources, blk:] + a[sources:, :blk])
                    - scale[f] * prev[1, f, :, lanes(r)]
                )
                p_out[0, f, :, lanes(r)] = real
                p_out[1, f, :, lanes(r)] = imag
                real16, imag16 = real.astype(jnp.bfloat16), imag.astype(jnp.bfloat16)
            t[0, f, :, lanes(r + reach)] = real
            t[1, f, :, lanes(r + reach)] = imag
            lhs[fr, :sources, :blk] = real16
            lhs[fr, :sources, blk:] = imag16
            lhs[fr, sources:, :blk] = imag16
            lhs[fr, sources:, blk:] = -real16
            squares = real * real + imag * imag
            return sums + jnp.sum(squares.reshape(sources // 8, 8, blk), axis=0)

        psq[f] = lax.fori_loop(0, rows, finish, jnp.zeros((8, blk), jnp.float32))

    def adjoint(g, carry):
        if first:
            arrive(g)
        for j in range(GROUP):
            i = g * GROUP + j
            f = item_f[i]
            weights = buf[item_buf[i]].reshape(2, 2 * blk, blk)
            out = jnp.dot(
                lhs[item_row[i]],
                jnp.concatenate([weights[0], weights[1]], axis=1),
                preferred_element_type=jnp.float32,
            )
            for index, half in ((item_a[i], out[:, :blk]), (item_b[i], out[:, blk:])):
                t[:, f, :, lanes(index)] += half.reshape(2, sources, blk)
        return carry

    lax.fori_loop(0, groups, adjoint, 0)


def operator_pass(counts, cols, blocks, start=None, field=None, prev=None, scale=None):
    freqs, rows, slots, _, blk, _ = blocks.shape
    first = start is not None
    sources = (start if first else prev).shape[2]
    reach = (slots - 1) // 2
    span = rows + 2 * reach
    pairs = (slots + 1) // 2
    items = freqs * rows * pairs
    dims = (freqs, rows, slots, blk, reach, sources)
    smem = pl.BlockSpec(memory_space=pltpu.SMEM)
    vmem = pl.BlockSpec(memory_space=pltpu.VMEM)
    hbm = pl.BlockSpec(memory_space=pl.ANY)
    t_shape = jax.ShapeDtypeStruct((2, freqs, sources, (span + 1) * blk), jnp.float32)
    psq_shape = jax.ShapeDtypeStruct((freqs, 8, blk), jnp.float32)
    listed = (items + GROUP,)
    scratch = [
        pltpu.VMEM((items, 2, 2, blk, blk), jnp.bfloat16),
        pltpu.VMEM((freqs * rows + 1, 2 * sources, 2 * blk), jnp.bfloat16),
        pltpu.SMEM(listed, jnp.int32),
        pltpu.SMEM(listed, jnp.int32),
        pltpu.SMEM(listed, jnp.int32),
        pltpu.SMEM(listed, jnp.int32),
        pltpu.SMEM(listed, jnp.int32),
        pltpu.SemaphoreType.DMA(((items + GROUP - 1) // GROUP,)),
    ]
    if first:
        args = (counts, cols, blocks, start)
        in_specs = [smem, smem, hbm, vmem]
        out_shape = (t_shape, psq_shape)
    else:
        args = (counts, cols, scale, blocks, field, prev)
        in_specs = [smem, smem, smem, hbm, vmem, vmem]
        out_shape = (jax.ShapeDtypeStruct(prev.shape, jnp.float32), t_shape, psq_shape)
        scratch += [
            pltpu.VMEM((2, freqs, sources, (span + 1) * blk), jnp.bfloat16),
            pltpu.VMEM((freqs * rows + 1, 2 * sources, 2 * blk), jnp.float32),
        ]
    return pl.pallas_call(
        functools.partial(pass_kernel, first, dims),
        out_shape=out_shape,
        in_specs=in_specs,
        out_specs=tuple(vmem for _ in out_shape),
        scratch_shapes=scratch,
        compiler_params=pltpu.CompilerParams(vmem_limit_bytes=56 * 1024 * 1024),
        name="first_adjoint" if first else "forward_adjoint",
    )(*args)


def body(up_time, down_blocks, block_cols, block_counts):
    freq_groups = lax.axis_size("freq")
    receiver_groups = lax.axis_size("rcv")
    shot_count, time_steps, receivers = up_time.shape
    local_freqs, local_blocks, slot_count, _, block_size, _ = down_blocks.shape
    local_rows = receivers // receiver_groups
    reach_blocks = (slot_count - 1) // 2
    rim = reach_blocks * block_size
    fourier = fourier_table(time_steps, freq_groups * local_freqs)
    fourier = fourier.reshape(time_steps, -1).T
    spectrum = jnp.stack(
        [
            jnp.dot(fourier, up_time[s], preferred_element_type=jnp.float32).astype(jnp.bfloat16)
            for s in range(shot_count)
        ],
        axis=1,
    )
    spectrum = spectrum.reshape(
        2, freq_groups, local_freqs, shot_count, receiver_groups, local_rows
    ).transpose(1, 4, 0, 2, 3, 5)
    spectrum = spectrum.reshape(
        freq_groups * receiver_groups, 2, local_freqs, shot_count, local_rows
    )
    received = lax.all_to_all(spectrum, ("freq", "rcv"), split_axis=0, concat_axis=0, tiled=True)
    right_side = received.transpose(1, 2, 0, 3, 4).reshape(2, local_freqs, -1, local_rows)
    counts = block_counts.reshape(-1)
    cols = block_cols.reshape(-1)
    ring = receiver_groups - 1
    up = [(i, i + 1) for i in range(ring)]
    down = [(i + 1, i) for i in range(ring)]

    def wide(value):
        return value[None, :, None, None]

    def own_part(t):
        lower = lax.ppermute(t[..., :rim], "rcv", down)
        upper = lax.ppermute(t[..., rim + local_rows : rim + local_rows + rim], "rcv", up)
        own = t[..., rim : rim + local_rows]
        own = own.at[..., :rim].add(upper)
        return own.at[..., local_rows - rim :].add(lower)

    def total(parts):
        return lax.psum(jnp.sum(parts, axis=tuple(range(1, parts.ndim))), "rcv")

    def square_sum(q):
        return lax.psum(jnp.sum(q * q, axis=(0, 2, 3)), "rcv")

    def extend(v):
        half = v.astype(jnp.bfloat16)
        below = lax.ppermute(half[..., local_rows - rim :], "rcv", up)
        above = lax.ppermute(half[..., :rim], "rcv", down)
        return jnp.concatenate(
            [below.astype(jnp.float32), v, above.astype(jnp.float32)], axis=-1
        )

    t, psq = operator_pass(counts, cols, down_blocks, start=right_side)
    beta = jnp.sqrt(total(psq) + EPSILON)
    q = own_part(t) / wide(beta)
    alpha = jnp.sqrt(square_sum(q) + EPSILON)
    v = q / wide(alpha)
    prev = right_side.astype(jnp.float32)
    w = v
    x = jnp.zeros_like(v)
    phibar = beta
    rhobar = alpha
    for iteration in range(ITERS):
        last = iteration == ITERS - 1
        prev, t, psq = operator_pass(
            counts, cols, down_blocks, field=extend(v), prev=prev, scale=alpha / beta
        )
        beta = jnp.sqrt(total(psq) + EPSILON)
        q = own_part(t) / wide(beta) - wide(beta) * v
        rho = jnp.sqrt(rhobar * rhobar + beta * beta)
        cosine = rhobar / rho
        sine = beta / rho
        phi = cosine * phibar
        phibar = sine * phibar
        x = x + wide(phi / rho) * w
        if last:
            return (x, wide(phibar * cosine) * q)
        alpha = jnp.sqrt(square_sum(q) + EPSILON)
        v = q / wide(alpha)
        theta = sine * alpha
        rhobar = -cosine * alpha
        w = v - wide(theta / rho) * w


def solution(mesh):
    return jax.shard_map(
        body,
        mesh=mesh,
        in_specs=(
            P(("freq", "rcv"), None, None),
            P("freq", "rcv", None, None, None, None),
            P("freq", "rcv", None),
            P("freq", "rcv"),
        ),
        out_specs=(P(None, "freq", None, "rcv"), P(None, "freq", None, "rcv")),
        check_vma=False,
    )
```

profile of v0, /device:TPU:7, one launch (start us, length us, event | category | flops | bytes accessed | tf_op | source)
XLA Modules:
  0.0 227.6 jit_solution(294546684876665301)
XLA Ops:
  0.8 5.5 %convolution_convert_fusion = bf16[16,20480]{1,0:T(8,128)(2,1)S(1)} fusion(bf16[1,256,20480]{2,1,0:T(8,128)(2,1)} %param.16, bf16[256,1,8]{0,2,1:T(8,128)(2,1)S(1)} %get-tuple-element.121, bf16[256,1,8]{0,2,1:T(8,128)(2,1)S(1)} %get-tuple-element.120), kind=kOutput, calls=%fused_computation | convolution fusion | flops 168103936 | bytes 11149312 | tf_op jit(solution)/shard_map/dot_general | solution.py:222
  6.5 1.3 copy.10
  7.8 6.4 %all-to-all-start = ((bf16[32,2,2,1,2560]{4,2,1,3,0:T(2,128)(2,1)}), bf16[32,2,2,1,2560]{4,2,1,3,0:T(2,128)(2,1)S(1)}, u32[]{:S(2)}, u32[]{:S(2)}) async-start(bf16[32,2,2,1,2560]{4,2,1,3,0:T(2,128)(2,1)} %bitcast.3), calls=%async_computation | async-start | bytes 1310720 | tf_op jit(solution)/shard_map/all_to_all | solution.py:233
  14.2 0.7 reshape.330.refs_0_
  15.0 0.7 reshape.331.refs_1_
  15.7 15.7 %all-to-all-done = bf16[32,2,2,1,2560]{4,2,1,3,0:T(2,128)(2,1)S(1)} async-done(((bf16[32,2,2,1,2560]{4,2,1,3,0:T(2,128)(2,1)}), bf16[32,2,2,1,2560]{4,2,1,3,0:T(2,128)(2,1)S(1)}, u32[]{:S(2)}, u32[]{:S(2)}) %all-to-all-start) | async-done | bytes 655392 | tf_op jit(solution)/shard_map/all_to_all | solution.py:233
  31.4 1.5 fusion.19
  32.8 15.9 %first_adjoint.1 = (f32[2,2,32,3968]{3,2,1,0:T(8,128)}, f32[2,8,128]{2,1,0:T(8,128)}) custom-call(s32[40]{0:T(128)} %reshape.330.refs_0_, s32[440]{0:T(512)} %reshape.331.refs_1_, bf16[2,20,11,2,128,128]{5,4,3,2,1,0:T(8,128)(2,1)} %refs_3_.3, bf16[2,2,32,2560]{3,2,1,0:T(8,128)(2,1)} %get-tuple-element.109.refs_3_), custom_call_target="tpu_custom_call" | custom-call | tf_op jit(solution)/shard_map/first_adjoint/pallas_call | solution.py:199
  48.7 1.1 fusion.27
  49.9 1.9 collective-permute-start
  51.9 13.4 %psum.35 = f32[2]{0:T(128)S(1)} all-reduce(f32[2]{0:T(128)S(1)} %reduce_sum.45), channel_id=1, replica_groups=mesh['freq'=4,'rcv'=8] {'rcv'}, use_global_device_ids=true, to_apply=%region_1.2 | all-reduce | flops 2 | bytes 16 | tf_op jit(solution)/shard_map/psum | solution.py:252
  65.3 2.7 %collective-permute-start.1 = (f32[2,2,32,640]{3,2,1,0:T(8,128)S(1)}, f32[2,2,32,640]{3,2,1,0:T(8,128)S(1)}, u32[]{:S(2)}, u32[]{:S(2)}) collective-permute-start(f32[2,2,32,640]{3,2,1,0:T(8,128)S(1)} %get-tuple-element.102), channel_id=1, source_target_pairs={{1,0},{2,1},{3,2},{4,3},{5,4},{6,5},{7,6},{9,8},{10,9},{11,10},{12... | collective-permute-start | bytes 983048 | tf_op jit(solution)/shard_map/ppermute | solution.py:245
  68.0 1.4 slice.216
  69.4 1.0 add_dynamic-update-slice_fusion.2
  70.5 3.3 %collective-permute-done.1 = f32[2,2,32,640]{3,2,1,0:T(8,128)S(1)} collective-permute-done((f32[2,2,32,640]{3,2,1,0:T(8,128)S(1)}, f32[2,2,32,640]{3,2,1,0:T(8,128)S(1)}, u32[]{:S(2)}, u32[]{:S(2)}) %collective-permute-start.1) | collective-permute-done | bytes 327712 | tf_op jit(solution)/shard_map/ppermute | solution.py:245
  73.8 0.4 multiply_reduce_fusion.1
  74.2 9.4 %psum.36 = f32[2]{0:T(128)S(1)} all-reduce(f32[2]{0:T(128)S(1)} %multiply_reduce_fusion.1), channel_id=1, replica_groups=mesh['freq'=4,'rcv'=8] {'rcv'}, use_global_device_ids=true, to_apply=%region_3.4 | all-reduce | flops 2 | bytes 16 | tf_op jit(solution)/shard_map/psum | solution.py:255
  83.6 0.6 fusion.16
  84.5 4.2 %collective-permute-start.2 = (bf16[2,2,32,640]{3,2,1,0:T(8,128)(2,1)S(1)}, bf16[2,2,32,640]{3,2,1,0:T(8,128)(2,1)S(1)}, u32[]{:S(2)}, u32[]{:S(2)}) collective-permute-start(bf16[2,2,32,640]{3,2,1,0:T(8,128)(2,1)S(1)} %get-tuple-element.110), channel_id=1, source_target_pairs={{0,1},{1,2},{2,3},{3,4},{4,5},{5,6},{6,7},{8,9},{9,10},{10,11},{11... | collective-permute-start | bytes 491528 | tf_op jit(solution)/shard_map/ppermute | solution.py:259
  88.7 3.7 %collective-permute-start.3 = (bf16[2,2,32,640]{3,2,1,0:T(8,128)(2,1)S(1)}, bf16[2,2,32,640]{3,2,1,0:T(8,128)(2,1)S(1)}, u32[]{:S(2)}, u32[]{:S(2)}) collective-permute-start(bf16[2,2,32,640]{3,2,1,0:T(8,128)(2,1)S(1)} %get-tuple-element.111), channel_id=1, source_target_pairs={{1,0},{2,1},{3,2},{4,3},{5,4},{6,5},{7,6},{9,8},{10,9},{11,10},{12... | collective-permute-start | bytes 491528 | tf_op jit(solution)/shard_map/ppermute | solution.py:260
  92.4 2.9 %collective-permute-done.3 = bf16[2,2,32,640]{3,2,1,0:T(8,128)(2,1)S(1)} collective-permute-done((bf16[2,2,32,640]{3,2,1,0:T(8,128)(2,1)S(1)}, bf16[2,2,32,640]{3,2,1,0:T(8,128)(2,1)S(1)}, u32[]{:S(2)}, u32[]{:S(2)}) %collective-permute-start.3) | collective-permute-done | bytes 163872 | tf_op jit(solution)/shard_map/ppermute | solution.py:260
  95.4 1.4 pad_maximum_fusion.refs_4_
  96.7 27.9 %forward_adjoint.2 = (f32[2,2,32,2560]{3,2,1,0:T(8,128)}, f32[2,2,32,3968]{3,2,1,0:T(8,128)}, f32[2,8,128]{2,1,0:T(8,128)}) custom-call(s32[40]{0:T(128)} %reshape.330.refs_0_, s32[440]{0:T(512)} %reshape.331.refs_1_, f32[2]{0:T(128)} %get-tuple-element.112.refs_2_, bf16[2,20,11,2,128,128]{5,4,3,2,1,0:T(8,128)(2,1)} %refs_3_.3, ...), custom_call_target="tpu_custom_call" | custom-call | tf_op jit(solution)/shard_map/forward_adjoint/pallas_call | solution.py:199
  124.7 1.1 fusion.26
  125.8 1.9 collective-permute-start.4
  127.9 14.2 %psum.37 = f32[2]{0:T(128)S(1)} all-reduce(f32[2]{0:T(128)S(1)} %reduce_sum.47), channel_id=1, replica_groups=mesh['freq'=4,'rcv'=8] {'rcv'}, use_global_device_ids=true, to_apply=%region_5.6 | all-reduce | flops 2 | bytes 16 | tf_op jit(solution)/shard_map/psum | solution.py:252
  142.0 2.7 %collective-permute-start.5 = (f32[2,2,32,640]{3,2,1,0:T(8,128)S(1)}, f32[2,2,32,640]{3,2,1,0:T(8,128)S(1)}, u32[]{:S(2)}, u32[]{:S(2)}) collective-permute-start(f32[2,2,32,640]{3,2,1,0:T(8,128)S(1)} %get-tuple-element.100), channel_id=1, source_target_pairs={{1,0},{2,1},{3,2},{4,3},{5,4},{6,5},{7,6},{9,8},{10,9},{11,10},{12... | collective-permute-start | bytes 983048 | tf_op jit(solution)/shard_map/ppermute | solution.py:245
  144.7 1.4 slice.223
  146.1 1.1 add_dynamic-update-slice_fusion.1
  147.2 3.2 %collective-permute-done.5 = f32[2,2,32,640]{3,2,1,0:T(8,128)S(1)} collective-permute-done((f32[2,2,32,640]{3,2,1,0:T(8,128)S(1)}, f32[2,2,32,640]{3,2,1,0:T(8,128)S(1)}, u32[]{:S(2)}, u32[]{:S(2)}) %collective-permute-start.5) | collective-permute-done | bytes 327712 | tf_op jit(solution)/shard_map/ppermute | solution.py:245
  150.5 0.4 multiply_reduce_fusion
  150.9 9.4 %psum.38 = f32[2]{0:T(128)S(1)} all-reduce(f32[2]{0:T(128)S(1)} %multiply_reduce_fusion), channel_id=1, replica_groups=mesh['freq'=4,'rcv'=8] {'rcv'}, use_global_device_ids=true, to_apply=%region_7.8 | all-reduce | flops 2 | bytes 16 | tf_op jit(solution)/shard_map/psum | solution.py:255
  160.4 0.6 fusion.18
  160.9 0.3 fusion.23
  161.3 4.2 %collective-permute-start.6 = (bf16[2,2,32,640]{3,2,1,0:T(8,128)(2,1)S(1)}, bf16[2,2,32,640]{3,2,1,0:T(8,128)(2,1)S(1)}, u32[]{:S(2)}, u32[]{:S(2)}) collective-permute-start(bf16[2,2,32,640]{3,2,1,0:T(8,128)(2,1)S(1)} %get-tuple-element.106), channel_id=1, source_target_pairs={{0,1},{1,2},{2,3},{3,4},{4,5},{5,6},{6,7},{8,9},{9,10},{10,11},{11... | collective-permute-start | bytes 491528 | tf_op jit(solution)/shard_map/ppermute | solution.py:259
  165.5 3.7 %collective-permute-start.7 = (bf16[2,2,32,640]{3,2,1,0:T(8,128)(2,1)S(1)}, bf16[2,2,32,640]{3,2,1,0:T(8,128)(2,1)S(1)}, u32[]{:S(2)}, u32[]{:S(2)}) collective-permute-start(bf16[2,2,32,640]{3,2,1,0:T(8,128)(2,1)S(1)} %get-tuple-element.107), channel_id=1, source_target_pairs={{1,0},{2,1},{3,2},{4,3},{5,4},{6,5},{7,6},{9,8},{10,9},{11,10},{12... | collective-permute-start | bytes 491528 | tf_op jit(solution)/shard_map/ppermute | solution.py:260
  169.2 2.9 %collective-permute-done.7 = bf16[2,2,32,640]{3,2,1,0:T(8,128)(2,1)S(1)} collective-permute-done((bf16[2,2,32,640]{3,2,1,0:T(8,128)(2,1)S(1)}, bf16[2,2,32,640]{3,2,1,0:T(8,128)(2,1)S(1)}, u32[]{:S(2)}, u32[]{:S(2)}) %collective-permute-start.7) | collective-permute-done | bytes 163872 | tf_op jit(solution)/shard_map/ppermute | solution.py:260
  172.1 1.4 pad_maximum_fusion.1.refs_4_
  173.5 28.0 %forward_adjoint.3 = (f32[2,2,32,2560]{3,2,1,0:T(8,128)}, f32[2,2,32,3968]{3,2,1,0:T(8,128)}, f32[2,8,128]{2,1,0:T(8,128)}) custom-call(s32[40]{0:T(128)} %reshape.330.refs_0_, s32[440]{0:T(512)} %reshape.331.refs_1_, f32[2]{0:T(128)} %get-tuple-element.118.refs_2_, bf16[2,20,11,2,128,128]{5,4,3,2,1,0:T(8,128)(2,1)} %refs_3_.3, ...), custom_call_target="tpu_custom_call" | custom-call | tf_op jit(solution)/shard_map/forward_adjoint/pallas_call | solution.py:199
  201.5 0.8 reduce_sum.49
  202.3 9.4 %psum.39 = f32[2]{0:T(128)S(1)} all-reduce(f32[2]{0:T(128)S(1)} %reduce_sum.49), channel_id=1, replica_groups=mesh['freq'=4,'rcv'=8] {'rcv'}, use_global_device_ids=true, to_apply=%region_9.10 | all-reduce | flops 2 | bytes 16 | tf_op jit(solution)/shard_map/psum | solution.py:252
  211.7 1.1 fusion.25
  212.9 4.2 %collective-permute-start.8 = (f32[2,2,32,640]{3,2,1,0:T(8,128)S(1)}, f32[2,2,32,640]{3,2,1,0:T(8,128)S(1)}, u32[]{:S(2)}, u32[]{:S(2)}) collective-permute-start(f32[2,2,32,640]{3,2,1,0:T(8,128)S(1)} %get-tuple-element.99), channel_id=1, source_target_pairs={{0,1},{1,2},{2,3},{3,4},{4,5},{5,6},{6,7},{8,9},{9,10},{10,11},{11... | collective-permute-start | bytes 983048 | tf_op jit(solution)/shard_map/ppermute | solution.py:246
  217.1 3.7 %collective-permute-start.9 = (f32[2,2,32,640]{3,2,1,0:T(8,128)S(1)}, f32[2,2,32,640]{3,2,1,0:T(8,128)S(1)}, u32[]{:S(2)}, u32[]{:S(2)}) collective-permute-start(f32[2,2,32,640]{3,2,1,0:T(8,128)S(1)} %get-tuple-element.98), channel_id=1, source_target_pairs={{1,0},{2,1},{3,2},{4,3},{5,4},{6,5},{7,6},{9,8},{10,9},{11,10},{12... | collective-permute-start | bytes 983048 | tf_op jit(solution)/shard_map/ppermute | solution.py:245
  220.8 1.4 slice.230
  222.2 1.1 add_dynamic-update-slice_fusion
  223.4 2.1 collective-permute-done.9
  225.6 2.0 subtract_multiply_fusion
  (37 shorter events, 1.4 us)
Async XLA Ops:
  6.4 7.8 %copy-start.5 = (s32[2,20]{1,0:T(2,128)S(1)}, s32[2,20]{1,0:T(2,128)}, u32[]{:S(2)}) copy-start(s32[2,20]{1,0:T(2,128)} %param.19) | copy-start | bytes 484
  6.4 8.4 %copy-start.2 = (s32[2,20,11]{1,0,2:T(2,128)S(1)}, s32[2,20,11]{1,0,2:T(2,128)}, u32[]{:S(2)}) copy-start(s32[2,20,11]{1,0,2:T(2,128)} %param.18) | copy-start | bytes 5284
  7.8 23.6 %all-to-all-start = ((bf16[32,2,2,1,2560]{4,2,1,3,0:T(2,128)(2,1)}), bf16[32,2,2,1,2560]{4,2,1,3,0:T(2,128)(2,1)S(1)}, u32[]{:S(2)}, u32[]{:S(2)}) async-start(bf16[32,2,2,1,2560]{4,2,1,3,0:T(2,128)(2,1)} %bitcast.3), calls=%async_computation | async-start | bytes 1310720 | tf_op jit(solution)/shard_map/all_to_all | solution.py:233
  48.7 3.1 %copy-start.4 = (f32[2,8,128]{2,1,0:T(8,128)S(1)}, f32[2,8,128]{2,1,0:T(8,128)}, u32[]{:S(2)}) copy-start(f32[2,8,128]{2,1,0:T(8,128)} %get-tuple-element.82) | copy-start | bytes 24580
  49.9 19.6 %collective-permute-start = (f32[2,2,32,640]{3,2,1,0:T(8,128)S(1)}, f32[2,2,32,640]{3,2,1,0:T(8,128)S(1)}, u32[]{:S(2)}, u32[]{:S(2)}) collective-permute-start(f32[2,2,32,640]{3,2,1,0:T(8,128)S(1)} %get-tuple-element.103), channel_id=1, source_target_pairs={{0,1},{1,2},{2,3},{3,4},{4,5},{5,6},{6,7},{8,9},{9,10},{10,11},{11... | collective-permute-start | bytes 983048 | tf_op jit(solution)/shard_map/ppermute | solution.py:246
  65.3 8.4 %collective-permute-start.1 = (f32[2,2,32,640]{3,2,1,0:T(8,128)S(1)}, f32[2,2,32,640]{3,2,1,0:T(8,128)S(1)}, u32[]{:S(2)}, u32[]{:S(2)}) collective-permute-start(f32[2,2,32,640]{3,2,1,0:T(8,128)S(1)} %get-tuple-element.102), channel_id=1, source_target_pairs={{1,0},{2,1},{3,2},{4,3},{5,4},{6,5},{7,6},{9,8},{10,9},{11,10},{12... | collective-permute-start | bytes 983048 | tf_op jit(solution)/shard_map/ppermute | solution.py:245
  84.5 7.9 %collective-permute-start.2 = (bf16[2,2,32,640]{3,2,1,0:T(8,128)(2,1)S(1)}, bf16[2,2,32,640]{3,2,1,0:T(8,128)(2,1)S(1)}, u32[]{:S(2)}, u32[]{:S(2)}) collective-permute-start(bf16[2,2,32,640]{3,2,1,0:T(8,128)(2,1)S(1)} %get-tuple-element.110), channel_id=1, source_target_pairs={{0,1},{1,2},{2,3},{3,4},{4,5},{5,6},{6,7},{8,9},{9,10},{10,11},{11... | collective-permute-start | bytes 491528 | tf_op jit(solution)/shard_map/ppermute | solution.py:259
  88.7 6.6 %collective-permute-start.3 = (bf16[2,2,32,640]{3,2,1,0:T(8,128)(2,1)S(1)}, bf16[2,2,32,640]{3,2,1,0:T(8,128)(2,1)S(1)}, u32[]{:S(2)}, u32[]{:S(2)}) collective-permute-start(bf16[2,2,32,640]{3,2,1,0:T(8,128)(2,1)S(1)} %get-tuple-element.111), channel_id=1, source_target_pairs={{1,0},{2,1},{3,2},{4,3},{5,4},{6,5},{7,6},{9,8},{10,9},{11,10},{12... | collective-permute-start | bytes 491528 | tf_op jit(solution)/shard_map/ppermute | solution.py:260
  124.7 3.1 %copy-start.3 = (f32[2,8,128]{2,1,0:T(8,128)S(1)}, f32[2,8,128]{2,1,0:T(8,128)}, u32[]{:S(2)}) copy-start(f32[2,8,128]{2,1,0:T(8,128)} %get-tuple-element.83) | copy-start | bytes 24580
  125.8 20.3 %collective-permute-start.4 = (f32[2,2,32,640]{3,2,1,0:T(8,128)S(1)}, f32[2,2,32,640]{3,2,1,0:T(8,128)}, u32[]{:S(2)}, u32[]{:S(2)}) collective-permute-start(f32[2,2,32,640]{3,2,1,0:T(8,128)S(1)} %get-tuple-element.101), channel_id=1, source_target_pairs={{0,1},{1,2},{2,3},{3,4},{4,5},{5,6},{6,7},{8,9},{9,10},{10,11},{11... | collective-permute-start | bytes 983048 | tf_op jit(solution)/shard_map/ppermute | solution.py:246
  142.0 8.4 %collective-permute-start.5 = (f32[2,2,32,640]{3,2,1,0:T(8,128)S(1)}, f32[2,2,32,640]{3,2,1,0:T(8,128)S(1)}, u32[]{:S(2)}, u32[]{:S(2)}) collective-permute-start(f32[2,2,32,640]{3,2,1,0:T(8,128)S(1)} %get-tuple-element.100), channel_id=1, source_target_pairs={{1,0},{2,1},{3,2},{4,3},{5,4},{6,5},{7,6},{9,8},{10,9},{11,10},{12... | collective-permute-start | bytes 983048 | tf_op jit(solution)/shard_map/ppermute | solution.py:245
  161.2 12.3 %copy-start = (f32[2,2,32,2560]{3,2,1,0:T(8,128)}, f32[2,2,32,2560]{3,2,1,0:T(8,128)S(1)}, u32[]{:S(2)}) copy-start(f32[2,2,32,2560]{3,2,1,0:T(8,128)S(1)} %get-tuple-element.95) | copy-start | bytes 3932164
  161.3 7.9 %collective-permute-start.6 = (bf16[2,2,32,640]{3,2,1,0:T(8,128)(2,1)S(1)}, bf16[2,2,32,640]{3,2,1,0:T(8,128)(2,1)S(1)}, u32[]{:S(2)}, u32[]{:S(2)}) collective-permute-start(bf16[2,2,32,640]{3,2,1,0:T(8,128)(2,1)S(1)} %get-tuple-element.106), channel_id=1, source_target_pairs={{0,1},{1,2},{2,3},{3,4},{4,5},{5,6},{6,7},{8,9},{9,10},{10,11},{11... | collective-permute-start | bytes 491528 | tf_op jit(solution)/shard_map/ppermute | solution.py:259
  165.5 6.6 %collective-permute-start.7 = (bf16[2,2,32,640]{3,2,1,0:T(8,128)(2,1)S(1)}, bf16[2,2,32,640]{3,2,1,0:T(8,128)(2,1)S(1)}, u32[]{:S(2)}, u32[]{:S(2)}) collective-permute-start(bf16[2,2,32,640]{3,2,1,0:T(8,128)(2,1)S(1)} %get-tuple-element.107), channel_id=1, source_target_pairs={{1,0},{2,1},{3,2},{4,3},{5,4},{6,5},{7,6},{9,8},{10,9},{11,10},{12... | collective-permute-start | bytes 491528 | tf_op jit(solution)/shard_map/ppermute | solution.py:260
  212.9 9.4 %collective-permute-start.8 = (f32[2,2,32,640]{3,2,1,0:T(8,128)S(1)}, f32[2,2,32,640]{3,2,1,0:T(8,128)S(1)}, u32[]{:S(2)}, u32[]{:S(2)}) collective-permute-start(f32[2,2,32,640]{3,2,1,0:T(8,128)S(1)} %get-tuple-element.99), channel_id=1, source_target_pairs={{0,1},{1,2},{2,3},{3,4},{4,5},{5,6},{6,7},{8,9},{9,10},{10,11},{11... | collective-permute-start | bytes 983048 | tf_op jit(solution)/shard_map/ppermute | solution.py:246
  217.1 8.4 %collective-permute-start.9 = (f32[2,2,32,640]{3,2,1,0:T(8,128)S(1)}, f32[2,2,32,640]{3,2,1,0:T(8,128)S(1)}, u32[]{:S(2)}, u32[]{:S(2)}) collective-permute-start(f32[2,2,32,640]{3,2,1,0:T(8,128)S(1)} %get-tuple-element.98), channel_id=1, source_target_pairs={{1,0},{2,1},{3,2},{4,3},{5,4},{6,5},{7,6},{9,8},{10,9},{11,10},{12... | collective-permute-start | bytes 983048 | tf_op jit(solution)/shard_map/ppermute | solution.py:245
  222.2 3.4 %copy-start.1 = (f32[2,2,32,2560]{3,2,1,0:T(8,128)S(1)}, f32[2,2,32,2560]{3,2,1,0:T(8,128)}, u32[]{:S(2)}) copy-start(f32[2,2,32,2560]{3,2,1,0:T(8,128)} %copy-done) | copy-start | bytes 3932164
where the time goes:
time: 228 us
  Pallas kernels  71.8 us (31%)
  blocking collectives  55.9 us (25%)
  starting transfers between devices  39.1 us (17%)
  waiting for transfers between devices  30.1 us (13%)
  other arithmetic  13.5 us (6%)
  local copies, waits for them, and re-layouts  10.7 us (5%)
  matrix products  5.45 us (2%)
    pallas_call x3, Pallas kernels, operator_pass(): pl.pallas_call(functools.partial(pass_kernel, first, dims), out_shape=out...  71.8 us
    psum x3, blocking collectives, total(): return lax.psum(jnp.sum(parts, axis=tuple(range(1, parts.ndim))), 'rcv')  37 us
    psum x2, blocking collectives, square_sum(): return lax.psum(jnp.sum(q * q, axis=(0, 2, 3)), 'rcv')  18.9 us
    all_to_all x1, waiting for transfers between devices, body(): lax.all_to_all(spectrum, ('freq', 'rcv'), split_axis=0, concat_axis=0, ti...  15.7 us
    ppermute x3, starting transfers between devices, own_part(): lower = lax.ppermute(t[..., :rim], 'rcv', down)  8.98 us
    ppermute x3, waiting for transfers between devices, own_part(): lower = lax.ppermute(t[..., :rim], 'rcv', down)  8.57 us
    ppermute x2, starting transfers between devices, extend(): below = lax.ppermute(half[..., local_rows - rim:], 'rcv', up)  8.37 us
    ppermute x3, starting transfers between devices, own_part(): lax.ppermute(t[..., rim + local_rows:rim + local_rows + rim], 'rcv', up)  8.03 us
  transfers between devices with their start and end apart: 11, of which 6 were waited for; matrix products, arithmetic and copies ran while one was open for 4% of the time, Pallas kernels for 0%

commit v1 on v0

--- a/solution.py
+++ b/solution.py
@@ -29,7 +29,7 @@
     if first:
         counts, cols, blocks, start, t, psq, buf, lhs, item_row, item_f, item_a, item_b, item_buf, sems = refs
     else:
-        (counts, cols, scale, blocks, field, prev, p_out, t, psq,
+        (counts, cols, blocks, field, stats, prev, p_out, t, psq,
          buf, lhs, item_row, item_f, item_a, item_b, item_buf, sems, zb, acc) = refs
     span = rows + 2 * reach
     pairs = (slots + 1) // 2
@@ -83,7 +83,12 @@
     t[...] = jnp.zeros_like(t)
     lhs[total_rows] = jnp.zeros(lhs.shape[1:], lhs.dtype)
     if not first:
-        zb[:, :, :, : span * blk] = field[...].astype(jnp.bfloat16)
+        inverse = 1.0 / stats[1]
+        ratio = stats[1] / stats[0]
+        for f in range(freqs):
+            for c in range(2):
+                scaled = field[c, f] * inverse[f : f + 1, :1]
+                zb[c, f, :, : span * blk] = scaled.astype(jnp.bfloat16)
         zb[:, :, :, span * blk :] = jnp.zeros((2, freqs, sources, blk), jnp.bfloat16)
         acc[...] = jnp.zeros_like(acc)
 
@@ -117,14 +122,14 @@
             else:
                 a = acc[fr]
                 real = (
-                    field[0, f, :, lanes(r + reach)]
+                    field[0, f, :, lanes(r + reach)] * inverse[f : f + 1, :]
                     + (a[:sources, :blk] - a[sources:, blk:])
-                    - scale[f] * prev[0, f, :, lanes(r)]
+                    - ratio[f : f + 1, :] * prev[0, f, :, lanes(r)]
                 )
                 imag = (
-                    field[1, f, :, lanes(r + reach)]
+                    field[1, f, :, lanes(r + reach)] * inverse[f : f + 1, :]
                     + (a[:sources, blk:] + a[sources:, :blk])
-                    - scale[f] * prev[1, f, :, lanes(r)]
+                    - ratio[f : f + 1, :] * prev[1, f, :, lanes(r)]
                 )
                 p_out[0, f, :, lanes(r)] = real
                 p_out[1, f, :, lanes(r)] = imag
@@ -159,7 +164,7 @@
     lax.fori_loop(0, groups, adjoint, 0)
 
 
-def operator_pass(counts, cols, blocks, start=None, field=None, prev=None, scale=None):
+def operator_pass(counts, cols, blocks, start=None, field=None, stats=None, prev=None):
     freqs, rows, slots, _, blk, _ = blocks.shape
     first = start is not None
     sources = (start if first else prev).shape[2]
@@ -189,8 +194,8 @@
         in_specs = [smem, smem, hbm, vmem]
         out_shape = (t_shape, psq_shape)
     else:
-        args = (counts, cols, scale, blocks, field, prev)
-        in_specs = [smem, smem, smem, hbm, vmem, vmem]
+        args = (counts, cols, blocks, field, stats, prev)
+        in_specs = [smem, smem, hbm, vmem, vmem, vmem]
         out_shape = (jax.ShapeDtypeStruct(prev.shape, jnp.float32), t_shape, psq_shape)
         scratch += [
             pltpu.VMEM((2, freqs, sources, (span + 1) * blk), jnp.bfloat16),
@@ -204,6 +209,186 @@
         scratch_shapes=scratch,
         compiler_params=pltpu.CompilerParams(vmem_limit_bytes=56 * 1024 * 1024),
         name="first_adjoint" if first else "forward_adjoint",
+    )(*args)
+
+
+def exchange_kernel(first, last, dims, *refs):
+    freqs, rows, blk, reach, peers = dims
+    t, psq, refs = refs[0], refs[1], refs[2:]
+    if not first:
+        before, stats_before, refs = refs[0], refs[1], refs[2:]
+    q, stats, refs = refs[0], refs[1], refs[2:]
+    (send_lo, send_hi, from_lo, from_hi, mine, theirs,
+     rim_send, rim_recv, sum_send, sum_recv) = refs
+    me = lax.axis_index("rcv")
+    two = 2 * reach * blk
+    rim = reach * blk
+    span = (rows + 2 * reach) * blk
+    has_lo = me > 0
+    has_hi = me < peers - 1
+
+    barrier = pltpu.get_barrier_semaphore()
+    for d in range(1, peers):
+        pl.semaphore_signal(
+            barrier, inc=1, device_id={"rcv": lax.rem(me + d, peers)},
+            device_id_type=pl.DeviceIdType.MESH,
+        )
+    send_lo[...] = t[:, :, :, :two].astype(jnp.bfloat16)
+    send_hi[...] = t[:, :, :, span - two : span].astype(jnp.bfloat16)
+
+    def to_row(parts):
+        rows_of = [jnp.sum(part, axis=0, keepdims=True) for part in parts]
+        rows_of.append(jnp.zeros((8 - len(parts), blk), jnp.float32))
+        return jnp.concatenate(rows_of, axis=0)
+
+    mine[0] = to_row([psq[f] for f in range(freqs)])
+    pl.semaphore_wait(barrier, peers - 1)
+
+    def sum_copy(k, d):
+        return pltpu.make_async_remote_copy(
+            src_ref=mine.at[k], dst_ref=theirs.at[k, d - 1],
+            send_sem=sum_send.at[k, d - 1], recv_sem=sum_recv.at[k, d - 1],
+            device_id={"rcv": lax.rem(me + d, peers)}, device_id_type=pl.DeviceIdType.MESH,
+        )
+
+    def lo_copy():
+        return pltpu.make_async_remote_copy(
+            src_ref=send_lo, dst_ref=from_hi, send_sem=rim_send.at[0], recv_sem=rim_recv.at[1],
+            device_id={"rcv": lax.rem(me + peers - 1, peers)}, device_id_type=pl.DeviceIdType.MESH,
+        )
+
+    def hi_copy():
+        return pltpu.make_async_remote_copy(
+            src_ref=send_hi, dst_ref=from_lo, send_sem=rim_send.at[1], recv_sem=rim_recv.at[0],
+            device_id={"rcv": lax.rem(me + 1, peers)}, device_id_type=pl.DeviceIdType.MESH,
+        )
+
+    for d in range(1, peers):
+        sum_copy(0, d).start()
+
+    @pl.when(has_lo)
+    def _():
+        lo_copy().start()
+
+    @pl.when(has_hi)
+    def _():
+        hi_copy().start()
+
+    @pl.when(jnp.logical_not(has_lo))
+    def _():
+        from_lo[...] = jnp.zeros_like(from_lo)
+
+    @pl.when(jnp.logical_not(has_hi))
+    def _():
+        from_hi[...] = jnp.zeros_like(from_hi)
+
+    def norm(k):
+        total = mine[k]
+        for d in range(1, peers):
+            sum_copy(k, d).wait_recv()
+        for d in range(1, peers):
+            total += theirs[k, d - 1]
+        value = jnp.sqrt(jnp.sum(total, axis=1, keepdims=True) + EPSILON)
+        return jnp.broadcast_to(value, (8, blk))
+
+    beta = norm(0)
+    stats[0] = beta
+    by_beta = 1.0 / beta
+    if not first:
+        pull = beta / stats_before[1]
+    sums = [jnp.zeros((8, blk), jnp.float32) for _ in range(freqs)]
+
+    def sweep(low, high, extra, offset):
+        own = low >= rim and high <= span - rim
+        if last and not own:
+            return
+        shift = rim if last else 0
+        for f in range(freqs):
+            for c in range(2):
+                value = t[c, f, :, low:high]
+                if extra is not None:
+                    value += extra[c, f, :, offset : offset + high - low].astype(jnp.float32)
+                value = value * by_beta[f : f + 1, :1]
+                if not first:
+                    value -= before[c, f, :, low:high] * pull[f : f + 1, :1]
+                q[c, f, :, low - shift : high - shift] = value
+                if own and not last:
+                    squares = value * value
+                    for j in range(0, high - low, blk):
+                        part = squares[:, j : j + blk]
+                        sums[f] = sums[f] + jnp.sum(part.reshape(-1, 8, blk), axis=0)
+
+    if span > 2 * two:
+        for low in range(two, span - two, rim):
+            sweep(low, min(low + rim, span - two), None, 0)
+
+    @pl.when(has_lo)
+    def _():
+        hi_like = pltpu.make_async_remote_copy(
+            src_ref=send_hi, dst_ref=from_lo, send_sem=rim_send.at[1], recv_sem=rim_recv.at[0],
+            device_id={"rcv": lax.rem(me + 1, peers)}, device_id_type=pl.DeviceIdType.MESH,
+        )
+        hi_like.wait_recv()
+
+    sweep(rim, two, from_lo, rim)
+
+    @pl.when(has_hi)
+    def _():
+        lo_copy().wait_recv()
+
+    sweep(span - two, span - rim, from_hi, 0)
+    if not last:
+        mine[1] = to_row(sums)
+        for d in range(1, peers):
+            sum_copy(1, d).start()
+        sweep(0, rim, from_lo, 0)
+        sweep(span - rim, span, from_hi, rim)
+        stats[1] = norm(1)
+    for d in range(1, peers):
+        sum_copy(0, d).wait_send()
+        if not last:
+            sum_copy(1, d).wait_send()
+
+    @pl.when(has_lo)
+    def _():
+        lo_copy().wait_send()
+
+    @pl.when(has_hi)
+    def _():
+        hi_copy().wait_send()
+
+
+def exchange(t, psq, before, stats_before, dims, last):
+    freqs, rows, blk, reach, peers = dims
+    first = before is None
+    sources = t.shape[2]
+    vmem = pl.BlockSpec(memory_space=pltpu.VMEM)
+    lanes = rows * blk if last else (rows + 2 * reach) * blk
+    args = (t, psq) if first else (t, psq, before, stats_before)
+    rim = pltpu.VMEM((2, freqs, sources, 2 * reach * blk), jnp.bfloat16)
+    return pl.pallas_call(
+        functools.partial(exchange_kernel, first, last, dims),
+        out_shape=(
+            jax.ShapeDtypeStruct((2, freqs, sources, lanes), jnp.float32),
+            jax.ShapeDtypeStruct((2, 8, blk), jnp.float32),
+        ),
+        in_specs=[vmem] * len(args),
+        out_specs=(vmem, vmem),
+        scratch_shapes=[
+            rim, rim, rim, rim,
+            pltpu.VMEM((2, 8, blk), jnp.float32),
+            pltpu.VMEM((2, peers - 1, 8, blk), jnp.float32),
+            pltpu.SemaphoreType.DMA((2,)),
+            pltpu.SemaphoreType.DMA((2,)),
+            pltpu.SemaphoreType.DMA((2, peers - 1)),
+            pltpu.SemaphoreType.DMA((2, peers - 1)),
+        ],
+        compiler_params=pltpu.CompilerParams(
+            collective_id=0 if first else (2 if last else 1),
+            has_side_effects=True,
+            vmem_limit_bytes=32 * 1024 * 1024,
+        ),
+        name="exchange",
     )(*args)
 
 
@@ -241,57 +426,72 @@
     def wide(value):
         return value[None, :, None, None]
 
-    def own_part(t):
+    def stats_of(beta, alpha):
+        rows = jnp.pad(jnp.stack([beta, alpha]), ((0, 0), (0, 8 - local_freqs)), constant_values=1.0)
+        return jnp.broadcast_to(rows[:, :, None], (2, 8, block_size))
+
+    def plain_exchange(t, psq, before, stats_before, last):
         lower = lax.ppermute(t[..., :rim], "rcv", down)
         upper = lax.ppermute(t[..., rim + local_rows : rim + local_rows + rim], "rcv", up)
-        own = t[..., rim : rim + local_rows]
-        own = own.at[..., :rim].add(upper)
-        return own.at[..., local_rows - rim :].add(lower)
-
-    def total(parts):
-        return lax.psum(jnp.sum(parts, axis=tuple(range(1, parts.ndim))), "rcv")
-
-    def square_sum(q):
-        return lax.psum(jnp.sum(q * q, axis=(0, 2, 3)), "rcv")
-
-    def extend(v):
-        half = v.astype(jnp.bfloat16)
-        below = lax.ppermute(half[..., local_rows - rim :], "rcv", up)
-        above = lax.ppermute(half[..., :rim], "rcv", down)
-        return jnp.concatenate(
-            [below.astype(jnp.float32), v, above.astype(jnp.float32)], axis=-1
-        )
+        q = t[..., rim : rim + local_rows]
+        q = q.at[..., :rim].add(upper)
+        q = q.at[..., local_rows - rim :].add(lower)
+        beta = jnp.sqrt(lax.psum(jnp.sum(psq, axis=(1, 2)), "rcv") + EPSILON)
+        q = q / wide(beta)
+        if before is not None:
+            own = before[..., rim : rim + local_rows]
+            q = q - wide(beta / stats_before[1, :local_freqs, 0]) * own
+        if last:
+            return q, stats_of(beta, beta)
+        alpha = jnp.sqrt(lax.psum(jnp.sum(q * q, axis=(0, 2, 3)), "rcv") + EPSILON)
+        below = lax.ppermute(q[..., local_rows - rim :], "rcv", up)
+        above = lax.ppermute(q[..., :rim], "rcv", down)
+        return jnp.concatenate([below, q, above], axis=-1), stats_of(beta, alpha)
+
+    def step(t, psq, before, stats_before, last):
+        if local_blocks < 2 * reach_blocks:
+            return plain_exchange(t, psq, before, stats_before, last)
+        dims = (local_freqs, local_blocks, block_size, reach_blocks, receiver_groups)
+        return exchange(t, psq, before, stats_before, dims, last)
 
     t, psq = operator_pass(counts, cols, down_blocks, start=right_side)
-    beta = jnp.sqrt(total(psq) + EPSILON)
-    q = own_part(t) / wide(beta)
-    alpha = jnp.sqrt(square_sum(q) + EPSILON)
-    v = q / wide(alpha)
     prev = right_side.astype(jnp.float32)
-    w = v
-    x = jnp.zeros_like(v)
-    phibar = beta
-    rhobar = alpha
+    q, stats = step(t, psq, None, None, False)
+    fields, norms = [q], [stats]
     for iteration in range(ITERS):
-        last = iteration == ITERS - 1
         prev, t, psq = operator_pass(
-            counts, cols, down_blocks, field=extend(v), prev=prev, scale=alpha / beta
-        )
-        beta = jnp.sqrt(total(psq) + EPSILON)
-        q = own_part(t) / wide(beta) - wide(beta) * v
+            counts, cols, down_blocks, field=q, stats=stats, prev=prev
+        )
+        q, stats = step(t, psq, q, stats, iteration == ITERS - 1)
+        fields.append(q)
+        norms.append(stats)
+
+    betas = [stats[0, :local_freqs, 0] for stats in norms]
+    alphas = [stats[1, :local_freqs, 0] for stats in norms]
+    phibar = betas[0]
+    rhobar = alphas[0]
+    weights = [jnp.zeros_like(phibar) for _ in range(ITERS)]
+    direction = [1.0 / alphas[0]]
+    for iteration in range(ITERS):
+        beta = betas[iteration + 1]
         rho = jnp.sqrt(rhobar * rhobar + beta * beta)
         cosine = rhobar / rho
         sine = beta / rho
         phi = cosine * phibar
         phibar = sine * phibar
-        x = x + wide(phi / rho) * w
-        if last:
-            return (x, wide(phibar * cosine) * q)
-        alpha = jnp.sqrt(square_sum(q) + EPSILON)
-        v = q / wide(alpha)
+        for i, part in enumerate(direction):
+            weights[i] = weights[i] + phi / rho * part
+        if iteration == ITERS - 1:
+            break
+        alpha = alphas[iteration + 1]
         theta = sine * alpha
         rhobar = -cosine * alpha
-        w = v - wide(theta / rho) * w
+        direction = [-theta / rho * part for part in direction] + [1.0 / alpha]
+    x = sum(
+        wide(weight) * field[..., rim : rim + local_rows]
+        for weight, field in zip(weights, fields)
+    )
+    return (x, wide(phibar * cosine) * q)
 
 
 def solution(mesh):

time: 228 us -> 151 us (0.66)
  the two profiles are of different devices: /device:TPU:7 before, /device:TPU:1 now
where the time goes in v1:
time: 151 us; the launch traced here: 153 us
  Pallas kernels  103 us (68%)
  waiting for transfers between devices  17.3 us (11%)
  local copies, waits for them, and re-layouts  14.2 us (9%)
  starting transfers between devices  7.1 us (5%)
  matrix products  5.45 us (4%)
  other arithmetic  4.22 us (3%)
    pallas_call x3, Pallas kernels, operator_pass(): pl.pallas_call(functools.partial(pass_kernel, first, dims), out_shape=out...  61.5 us
    pallas_call x3, Pallas kernels, exchange(): pl.pallas_call(functools.partial(exchange_kernel, first, last, dims), out...  42 us
    all_to_all x1, waiting for transfers between devices, body(): lax.all_to_all(spectrum, ('freq', 'rcv'), split_axis=0, concat_axis=0, ti...  17.3 us
    unnamed x34, local copies, waits for them, and re-layouts  11.3 us
    all_to_all x1, starting transfers between devices, body(): lax.all_to_all(spectrum, ('freq', 'rcv'), split_axis=0, concat_axis=0, ti...  7.1 us
    dot_general x1, matrix products, body(): jnp.dot(fourier, up_time[s], preferred_element_type=jnp.float32)  5.45 us
  transfers between devices with their start and end apart: 1, of which 1 were waited for; matrix products, arithmetic and copies ran while one was open for 1% of the time, Pallas kernels for 0%

profile of v1, /device:TPU:1, one launch (start us, length us, event | category | flops | bytes accessed | tf_op | source)
XLA Modules:
  0.0 152.6 jit_solution(16064526855586179089)
XLA Ops:
  0.6 0.1 multiply_convert_fusion.1
  0.8 5.5 %convolution_convert_fusion = bf16[16,20480]{1,0:T(8,128)(2,1)S(1)} fusion(bf16[1,256,20480]{2,1,0:T(8,128)(2,1)} %param.4, bf16[256,1,8]{0,2,1:T(8,128)(2,1)S(1)} %get-tuple-element.41, bf16[256,1,8]{0,2,1:T(8,128)(2,1)S(1)} %get-tuple-element.40), kind=kOutput, calls=%fused_computation | convolution fusion | flops 168103936 | bytes 11149312 | tf_op jit(solution)/shard_map/dot_general | solution.py:407
  6.2 0.2 copy.12
  6.4 0.0 copy-start.14
  6.4 0.0 copy-start.15
  6.5 1.3 copy.10
  7.8 7.1 %all-to-all-start = ((bf16[32,2,2,1,2560]{4,2,1,3,0:T(2,128)(2,1)}), bf16[32,2,2,1,2560]{4,2,1,3,0:T(2,128)(2,1)S(1)}, u32[]{:S(2)}, u32[]{:S(2)}) async-start(bf16[32,2,2,1,2560]{4,2,1,3,0:T(2,128)(2,1)} %bitcast.3), calls=%async_computation | async-start | bytes 1310720 | tf_op jit(solution)/shard_map/all_to_all | solution.py:418
  14.9 0.0 copy-done.14
  14.9 0.1 copy.9
  15.0 0.7 reshape.230.refs_1_
  15.7 0.0 copy-done.15
  15.7 0.6 reshape.229.refs_0_
  16.3 17.3 %all-to-all-done = bf16[32,2,2,1,2560]{4,2,1,3,0:T(2,128)(2,1)S(1)} async-done(((bf16[32,2,2,1,2560]{4,2,1,3,0:T(2,128)(2,1)}), bf16[32,2,2,1,2560]{4,2,1,3,0:T(2,128)(2,1)S(1)}, u32[]{:S(2)}, u32[]{:S(2)}) %all-to-all-start) | async-done | bytes 655392 | tf_op jit(solution)/shard_map/all_to_all | solution.py:418
  33.6 1.5 fusion.13
  35.0 13.6 %first_adjoint.1 = (f32[2,2,32,3968]{3,2,1,0:T(8,128)}, f32[2,8,128]{2,1,0:T(8,128)}) custom-call(s32[40]{0:T(128)} %reshape.229.refs_0_, s32[440]{0:T(512)} %reshape.230.refs_1_, bf16[2,20,11,2,128,128]{5,4,3,2,1,0:T(8,128)(2,1)} %refs_2_.5, bf16[2,2,32,2560]{3,2,1,0:T(8,128)(2,1)} %get-tuple-element.39.refs_3_), custom_call_target="tpu_custom_call" | custom-call | tf_op jit(solution)/shard_map/first_adjoint/pallas_call | solution.py:204
  48.6 0.0 copy-start.6
  48.6 1.6 %copy-done.6 = f32[2,2,32,3968]{3,2,1,0:T(8,128)S(1)} copy-done((f32[2,2,32,3968]{3,2,1,0:T(8,128)S(1)}, f32[2,2,32,3968]{3,2,1,0:T(8,128)}, u32[]{:S(2)}) %copy-start.6) | copy-done | bytes 2031640
  50.2 0.0 copy-start.13
  50.2 0.7 copy-done.13
  50.9 14.2 %exchange.3 = (f32[2,2,32,3840]{3,2,1,0:T(8,128)S(1)}, f32[2,8,128]{2,1,0:T(8,128)S(1)}) custom-call(f32[2,2,32,3968]{3,2,1,0:T(8,128)S(1)} %copy-done.6, f32[2,8,128]{2,1,0:T(8,128)S(1)} %copy-done.13), custom_call_target="tpu_custom_call" | custom-call | tf_op jit(solution)/shard_map/exchange/pallas_call | solution.py:369
  65.1 0.0 copy-start
  65.1 1.3 copy-done
  66.3 0.0 copy-start.7
  66.3 0.6 copy-done.7
  66.9 0.0 copy-start.1
  66.9 0.0 copy-start.8
  66.9 23.9 %forward_adjoint.2 = (f32[2,2,32,2560]{3,2,1,0:T(8,128)}, f32[2,2,32,3968]{3,2,1,0:T(8,128)}, f32[2,8,128]{2,1,0:T(8,128)}) custom-call(s32[40]{0:T(128)} %reshape.229.refs_0_, s32[440]{0:T(512)} %reshape.230.refs_1_, bf16[2,20,11,2,128,128]{5,4,3,2,1,0:T(8,128)(2,1)} %refs_2_.5, f32[2,2,32,3840]{3,2,1,0:T(8,128)} %copy-done, f32[2,8,128]{2,1,0:T(8,128)} %copy-done.7, ...), custom_call_target="tpu_custom_call" | custom-call | tf_op jit(solution)/shard_map/forward_adjoint/pallas_call | solution.py:204
  90.9 0.0 copy-done.1
  90.9 0.0 copy-done.8
  90.9 0.0 copy-start.5
  90.9 1.6 %copy-done.5 = f32[2,2,32,3968]{3,2,1,0:T(8,128)S(1)} copy-done((f32[2,2,32,3968]{3,2,1,0:T(8,128)S(1)}, f32[2,2,32,3968]{3,2,1,0:T(8,128)}, u32[]{:S(2)}) %copy-start.5) | copy-done | bytes 2031640
  92.5 0.0 copy-start.12
  92.5 0.7 copy-done.12
  93.1 16.0 %exchange.4 = (f32[2,2,32,3840]{3,2,1,0:T(8,128)S(1)}, f32[2,8,128]{2,1,0:T(8,128)S(1)}) custom-call(f32[2,2,32,3968]{3,2,1,0:T(8,128)S(1)} %copy-done.5, f32[2,8,128]{2,1,0:T(8,128)S(1)} %copy-done.12, f32[2,2,32,3840]{3,2,1,0:T(8,128)S(1)} %copy-done.1, f32[2,8,128]{2,1,0:T(8,128)S(1)} %copy-done.8), custom_call_target="tpu_custom_call" | custom-call | tf_op jit(solution)/shard_map/exchange/pallas_call | solution.py:369
  109.1 0.0 copy-start.2
  109.1 1.3 copy-done.2
  110.4 0.1 slice_reduce_fusion.3
  110.5 0.4 copy-done.9
  111.0 23.9 %forward_adjoint.3 = (f32[2,2,32,2560]{3,2,1,0:T(8,128)}, f32[2,2,32,3968]{3,2,1,0:T(8,128)}, f32[2,8,128]{2,1,0:T(8,128)}) custom-call(s32[40]{0:T(128)} %reshape.229.refs_0_, s32[440]{0:T(512)} %reshape.230.refs_1_, bf16[2,20,11,2,128,128]{5,4,3,2,1,0:T(8,128)(2,1)} %refs_2_.5, f32[2,2,32,3840]{3,2,1,0:T(8,128)} %copy-done.2, f32[2,8,128]{2,1,0:T(8,128)} %copy-done.9, ...), custom_call_target="tpu_custom_call" | custom-call | tf_op jit(solution)/shard_map/forward_adjoint/pallas_call | solution.py:204
  134.9 0.0 copy-done.3
  134.9 0.0 copy-start.4
  134.9 1.6 %copy-done.4 = f32[2,2,32,3968]{3,2,1,0:T(8,128)S(1)} copy-done((f32[2,2,32,3968]{3,2,1,0:T(8,128)S(1)}, f32[2,2,32,3968]{3,2,1,0:T(8,128)}, u32[]{:S(2)}) %copy-start.4) | copy-done | bytes 2031640
  136.5 0.7 copy-done.10
  137.2 0.7 copy-done.11
  137.9 11.9 %exchange.5 = (f32[2,2,32,2560]{3,2,1,0:T(8,128)S(1)}, f32[2,8,128]{2,1,0:T(8,128)S(1)}) custom-call(f32[2,2,32,3968]{3,2,1,0:T(8,128)S(1)} %copy-done.4, f32[2,8,128]{2,1,0:T(8,128)S(1)} %copy-done.11, f32[2,2,32,3840]{3,2,1,0:T(8,128)S(1)} %copy-done.3, f32[2,8,128]{2,1,0:T(8,128)S(1)} %copy-done.10), custom_call_target="tpu_custom_call" | custom-call | tf_op jit(solution)/shard_map/exchange/pallas_call | solution.py:369
  149.8 0.1 slice_reduce_fusion.2
  150.0 1.3 broadcast_multiply_fusion
  151.3 1.3 multiply_add_fusion
  (8 shorter events, 0.1 us)
Async XLA Ops:
  6.4 8.5 %copy-start.14 = (s32[2,20,11]{1,0,2:T(2,128)S(1)}, s32[2,20,11]{1,0,2:T(2,128)}, u32[]{:S(2)}) copy-start(s32[2,20,11]{1,0,2:T(2,128)} %param.6) | copy-start | bytes 5284
  6.4 9.3 %copy-start.15 = (s32[2,20]{1,0:T(2,128)S(1)}, s32[2,20]{1,0:T(2,128)}, u32[]{:S(2)}) copy-start(s32[2,20]{1,0:T(2,128)} %param.7) | copy-start | bytes 484
  7.8 25.8 %all-to-all-start = ((bf16[32,2,2,1,2560]{4,2,1,3,0:T(2,128)(2,1)}), bf16[32,2,2,1,2560]{4,2,1,3,0:T(2,128)(2,1)S(1)}, u32[]{:S(2)}, u32[]{:S(2)}) async-start(bf16[32,2,2,1,2560]{4,2,1,3,0:T(2,128)(2,1)} %bitcast.3), calls=%async_computation | async-start | bytes 1310720 | tf_op jit(solution)/shard_map/all_to_all | solution.py:418
  48.6 1.6 %copy-start.6 = (f32[2,2,32,3968]{3,2,1,0:T(8,128)S(1)}, f32[2,2,32,3968]{3,2,1,0:T(8,128)}, u32[]{:S(2)}) copy-start(f32[2,2,32,3968]{3,2,1,0:T(8,128)} %get-tuple-element.15.refs_0_) | copy-start | bytes 6094852
  50.2 0.7 copy-start.13
  65.1 1.3 copy-start
  66.3 0.6 copy-start.7
  66.9 24.0 %copy-start.1 = (f32[2,2,32,3840]{3,2,1,0:T(8,128)S(1)}, f32[2,2,32,3840]{3,2,1,0:T(8,128)}, u32[]{:S(2)}) copy-start(f32[2,2,32,3840]{3,2,1,0:T(8,128)} %copy-done) | copy-start | bytes 5898244
  66.9 24.0 %copy-start.8 = (f32[2,8,128]{2,1,0:T(8,128)S(1)}, f32[2,8,128]{2,1,0:T(8,128)}, u32[]{:S(2)}) copy-start(f32[2,8,128]{2,1,0:T(8,128)} %copy-done.7) | copy-start | bytes 24580
  90.9 1.6 %copy-start.5 = (f32[2,2,32,3968]{3,2,1,0:T(8,128)S(1)}, f32[2,2,32,3968]{3,2,1,0:T(8,128)}, u32[]{:S(2)}) copy-start(f32[2,2,32,3968]{3,2,1,0:T(8,128)} %get-tuple-element.19.refs_0_) | copy-start | bytes 6094852
  92.5 0.7 copy-start.12
  109.1 1.3 copy-start.2
  110.4 0.6 copy-start.9
  111.0 24.0 %copy-start.3 = (f32[2,2,32,3840]{3,2,1,0:T(8,128)S(1)}, f32[2,2,32,3840]{3,2,1,0:T(8,128)}, u32[]{:S(2)}) copy-start(f32[2,2,32,3840]{3,2,1,0:T(8,128)} %copy-done.2) | copy-start | bytes 5898244
  134.9 1.6 %copy-start.4 = (f32[2,2,32,3968]{3,2,1,0:T(8,128)S(1)}, f32[2,2,32,3968]{3,2,1,0:T(8,128)}, u32[]{:S(2)}) copy-start(f32[2,2,32,3968]{3,2,1,0:T(8,128)} %get-tuple-element.24.refs_0_) | copy-start | bytes 6094852
  136.5 0.7 copy-start.10
  137.2 0.7 copy-start.11
